TPU v7x, 256 devices: a whole 4x4x8 slice. The times are simulated.
256 devices in a mesh: tm: 16 (over x, y), space: 16 (over z, core).
Axes of the slice: x: 4, y: 4, z: 8, core: 2. Of those that a mesh axis runs over, the one named last changes fastest.
Arguments:
- queries: bfloat16 [32, 32, 32, 2240], P('tm', 'space'), may hold values from -6 to 6
- keys: bfloat16 [32, 32, 32, 2240], P('tm', 'space'), may hold values from -6 to 6
- values: bfloat16 [32, 32, 32, 2240], P('tm', 'space'), may hold values from -6 to 6
- out_grad: bfloat16 [32, 32, 32, 2240], P('tm', 'space'), may hold values from -6 to 6
- block_start: int32 [32], P('tm'), may hold values 0 or 1
- conv_input: bfloat16 [32, 32, 32, 5632], P('tm', 'space'), may hold values from -6 to 6
- conv_grad: bfloat16 [32, 32, 32, 5632], P('tm', 'space'), may hold values from -6 to 6
- conv_weight: float32 [9, 5632], replicated, may hold values from -2 to 2
Outputs:
- query_grad: bfloat16 [32, 32, 32, 2240], P('tm', 'space')
- key_grad: bfloat16 [32, 32, 32, 2240], P('tm', 'space')
- value_grad: bfloat16 [32, 32, 32, 2240], P('tm', 'space')
- input_grad: bfloat16 [32, 32, 32, 5632], P('tm', 'space')
- kernel_grad: float32 [9, 5632], replicated
All inputs are finite; a program needn't handle non-finite values. No bound on the sum of `block_start` on one device may be relied on, other than what follows from the above.
Results may differ from a plain program's by a relative error of at most 0.0088.
Values may be sent and summed in bfloat16 or wider, within the bound.
A program may use at most 128 MiB of HBM per device.

v0:
```python
import math
import jax
import jax.numpy as jnp
from jax import lax
from jax.sharding import PartitionSpec as P

HEADS = 20
HD = 112
highest = lax.Precision.HIGHEST


def with_halo(cells, sides, width):
    for axis, dim in sides:
        count = lax.axis_size(axis)
        ends = count - 1
        head = lax.slice_in_dim(cells, 0, width, axis=dim)
        tail = lax.slice_in_dim(cells, cells.shape[dim] - width, cells.shape[dim], axis=dim)
        cells = jnp.concatenate(
            [
                lax.ppermute(tail, axis, [(i, (i + 1) % count) for i in range(ends)]),
                cells,
                lax.ppermute(head, axis, [((i + 1) % count, i) for i in range(ends)]),
            ],
            axis=dim,
        )
    return cells


def prefix(part, axis, combine, identity, reverse):
    count = lax.axis_size(axis)
    place = lax.axis_index(axis)
    ahead = count - 1 - place if reverse else place
    gathered = jax.tree.map(lambda a: lax.all_gather(a, axis), part)
    state = jax.tree.map(lambda a, e: jnp.zeros_like(a) + jnp.asarray(e, a.dtype), part, identity)

    def one(turn, state):
        source = count - 1 - turn if reverse else turn
        return combine(
            state, jax.tree.map(lambda a: lax.dynamic_index_in_dim(a, source, 0, False), gathered)
        )

    return lax.fori_loop(0, ahead, one, state)


def lifted(x):
    widened = x.astype(jnp.float32)
    return jnp.where(widened > 0, widened + 1.0, jnp.exp(jnp.minimum(widened, 0.0)))


def slopes(x):
    widened = x.astype(jnp.float32)
    return jnp.where(widened > 0, 1.0, jnp.exp(jnp.minimum(widened, 0.0)))


def visibility(block_start, count):
    position = jnp.arange(count, dtype=jnp.int32)
    starts = jnp.where(position == 0, 1, block_start)
    block_ids = jnp.cumsum(starts)
    return (block_ids[None, :] <= block_ids[:, None]).astype(jnp.float32)


def add_pair(earlier, later):
    return (earlier[0] + later[0], earlier[1] + later[1])


def body(queries, keys, values, out_grad, block_start, conv_input, conv_grad, conv_weight):
    frames, rows, cols, width = queries.shape
    heads = HEADS
    depth = HD
    head_shape = (frames, rows * cols, heads, depth)
    q_feat = lifted(queries).astype(jnp.bfloat16).reshape(head_shape)
    k_feat = lifted(keys).astype(jnp.bfloat16).reshape(head_shape)
    v_heads = values.reshape(head_shape)
    visible = visibility(block_start, frames)
    rimmed = with_halo(conv_grad, (("space", 1),), 1)
    states = jnp.einsum("fnhd,fnhe->fhde", k_feat, v_heads, preferred_element_type=jnp.float32)
    sums = jnp.sum(k_feat.astype(jnp.float32), axis=1)
    states, sums = lax.psum((states, sums), "space")
    earlier = prefix(
        (jnp.sum(states, axis=0), jnp.sum(sums, axis=0)),
        "tm",
        add_pair,
        (jnp.zeros(states.shape[1:], jnp.float32), jnp.zeros(sums.shape[1:], jnp.float32)),
        False,
    )
    seen_states = jnp.einsum("fg,ghde->fhde", visible, states, precision=highest) + earlier[0][None]
    seen_sums = jnp.einsum("fg,ghd->fhd", visible, sums, precision=highest) + earlier[1][None]
    q_wide = q_feat.astype(jnp.float32)
    grad_wide = out_grad.reshape(head_shape).astype(jnp.float32)
    numer = jnp.einsum("fnhd,fhde->fnhe", q_wide, seen_states, precision=highest)
    denominator = jnp.einsum("fnhd,fhd->fnh", q_wide, seen_sums, precision=highest)
    output = numer / denominator[..., None]
    numer_grad = (grad_wide / denominator[..., None]).astype(jnp.bfloat16)
    denom_grad = -jnp.sum(grad_wide * output, axis=-1) / denominator
    q_grad = jnp.einsum(
        "fnhe,fhde->fnhd", numer_grad.astype(jnp.float32), seen_states, precision=highest
    )
    q_grad = (q_grad + denom_grad[..., None] * seen_sums[:, None]) * slopes(
        queries.reshape(head_shape)
    )
    grad_states = jnp.einsum(
        "fnhd,fnhe->fhde", q_feat, numer_grad, preferred_element_type=jnp.float32
    )
    grad_sums = jnp.einsum("fnhd,fnh->fhd", q_wide, denom_grad, precision=highest)
    grad_states, grad_sums = lax.psum((grad_states, grad_sums), "space")
    later = prefix(
        (jnp.sum(grad_states, axis=0), jnp.sum(grad_sums, axis=0)),
        "tm",
        add_pair,
        (
            jnp.zeros(grad_states.shape[1:], jnp.float32),
            jnp.zeros(grad_sums.shape[1:], jnp.float32),
        ),
        True,
    )
    seen_grads = (
        jnp.einsum("fg,fhde->ghde", visible, grad_states, precision=highest) + later[0][None]
    )
    seen_gsums = jnp.einsum("fg,fhd->ghd", visible, grad_sums, precision=highest) + later[1][None]
    k_grad = jnp.einsum(
        "fnhe,fhde->fnhd", v_heads.astype(jnp.float32), seen_grads, precision=highest
    )
    k_grad = (k_grad + seen_gsums[:, None]) * slopes(keys.reshape(head_shape))
    v_grad = jnp.einsum(
        "fnhd,fhde->fnhe", k_feat.astype(jnp.float32), seen_grads, precision=highest
    )
    out_shape = (frames, rows, cols, width)
    padded = jnp.pad(rimmed.astype(jnp.float32), ((0, 0), (0, 0), (1, 1), (0, 0)))
    input_wide = conv_input.astype(jnp.float32)
    accum = jnp.zeros(conv_grad.shape, jnp.float32)
    kernel_rows = []
    for i in range(3):
        for j in range(3):
            window = padded[:, 2 - i : 2 - i + rows, 2 - j : 2 - j + cols]
            accum = accum + conv_weight[3 * i + j] * window
            kernel_rows.append(jnp.sum(window * input_wide, axis=(0, 1, 2)))
    kernel_total = lax.psum(jnp.stack(kernel_rows), ("tm", "space"))
    tokens_all = frames * rows * cols * lax.axis_size("tm") * lax.axis_size("space")
    kernel_grad = kernel_total * (1.0 / math.sqrt(tokens_all))
    return (
        q_grad.astype(jnp.bfloat16).reshape(out_shape),
        k_grad.astype(jnp.bfloat16).reshape(out_shape),
        v_grad.astype(jnp.bfloat16).reshape(out_shape),
        accum.astype(jnp.bfloat16),
        kernel_grad,
    )


def solution(mesh):
    placed = (
        P("tm", "space", None, None),
        P("tm", "space", None, None),
        P("tm", "space", None, None),
        P("tm", "space", None, None),
        P("tm"),
        P("tm", "space", None, None),
        P("tm", "space", None, None),
        P(),
    )
    return jax.shard_map(
        body,
        mesh=mesh,
        in_specs=placed,
        out_specs=(
            P("tm", "space", None, None),
            P("tm", "space", None, None),
            P("tm", "space", None, None),
            P("tm", "space", None, None),
            P(),
        ),
        check_vma=False,
    )
```

profile of v0, /device:TPU:1, one launch (start us, length us, event | category | flops | bytes accessed | tf_op | source)
XLA Modules:
  0.0 849.6 jit_solution(3635706949680957188)
XLA Ops:
  7.2 2.0 reshape.94
  9.2 2.7 convert_reduce_fusion
  12.0 0.8 reshape.93
  12.8 1.9 fusion.78
  14.8 119.5 %all-reduce.5.cloned.1.call-done = f32[2,20,112,112]{3,2,1,0:T(8,128)} async-done(((f32[2,20,112,112]{3,2,1,0:T(8,128)}), f32[2,20,112,112]{3,2,1,0:T(8,128)}) %all-reduce.5.cloned.1.call-update) | async-done | bytes 2007056 | tf_op jit(solution)/shard_map/psum | solution.py:78
  134.3 2.9 reduce_sum.137
  137.3 1.2 fusion.93
  138.6 2.3 collective-permute-start.1
  140.8 3.3 collective-permute-start
  144.4 2.0 reshape.99
  146.4 1.3 fusion.74
  147.8 0.8 reshape.95
  148.6 44.8 %psum.36 = f32[2,20,112]{2,0,1:T(2,128)S(1)} all-reduce(f32[2,20,112]{2,0,1:T(2,128)S(1)} %copy.57), channel_id=1, replica_groups=mesh['tm'=16,'space'=16] {'space'}, use_global_device_ids=true, to_apply=%region_4.5 | all-reduce | flops 4480 | bytes 35840 | tf_op jit(solution)/shard_map/psum | solution.py:78
  193.5 22.7 %all-gather.4 = f32[16,20,112]{2,1,0:T(8,128)} all-gather(f32[1,20,112]{2,1,0:T(8,128)S(1)} %bitcast.88), channel_id=3, replica_groups=mesh['tm'=16,'space'=16] {'tm'}, dimensions={0}, use_global_device_ids=true | all-gather | bytes 152320 | tf_op jit(solution)/shard_map/all_gather | solution.py:33
  216.2 47.2 %all-gather.9.cloned.1.call-done = f32[320,112,112]{2,1,0:T(8,128)} async-done(((f32[20,112,112]{2,1,0:T(8,128)}), f32[320,112,112]{2,1,0:T(8,128)}) %all-gather.9.cloned.1.call-update) | async-done | bytes 16056336 | tf_op jit(solution)/shard_map/all_gather | solution.py:33
  263.8 1.1 fusion.86
  264.9 3.7 fusion.82
  268.8 1.9 maximum_convert_fusion
  270.7 3.6 fusion.8
  274.5 1.6 stack.39
  276.4 140.1 %all-reduce.7.cloned.1.call-done = f32[2,20,112,112]{3,2,1,0:T(8,128)} async-done(((f32[2,20,112,112]{3,2,1,0:T(8,128)}), f32[2,20,112,112]{3,2,1,0:T(8,128)}) %all-reduce.7.cloned.1.call-update) | async-done | bytes 2007056 | tf_op jit(solution)/shard_map/psum | solution.py:105
  416.5 3.0 reduce_sum.142
  419.5 1.9 select_n.43
  421.4 1.9 select_n.45
  423.9 12.4 %add_convert_fusion = bf16[2,2,32,5632]{3,2,1,0:T(8,128)(2,1)} fusion(f32[2,4,32,5632]{3,2,1,0:T(8,128)} %copy-done, f32[5632]{0:T(1024)S(1)} %get-tuple-element.140, f32[5632]{0:T(1024)S(1)} %get-tuple-element.141, f32[5632]{0:T(1024)S(1)} %get-tuple-element.134, f32[5632]{0:T(1024)S(1)} %get-tuple-element.135, f32[5632]{0:T(1024)S(1)} %get-tuple-element.136, ...), kind=kLoop, calls=%fused_computation.29 | loop fusion | flops 12976128 | bytes 16062464 | tf_op jit(solution)/shard_map/convert_element_type | solution.py:144
  436.3 233.9 %all-reduce.9.cloned.1.call-done = f32[9,5632]{1,0:T(8,128)} async-done(((f32[9,5632]{1,0:T(8,128)}), f32[9,5632]{1,0:T(8,128)}) %all-reduce.9.cloned.1.call-update) | async-done | bytes 202768 | tf_op jit(solution)/shard_map/psum | solution.py:137
  670.2 1.8 broadcast_multiply_fusion
  672.0 6.7 fusion.48
  678.7 1.6 fusion.66
  680.4 2.8 fusion.54
  683.6 1.4 reshape.96
  685.7 44.5 %psum.38 = f32[2,20,112]{2,0,1:T(2,128)S(1)} all-reduce(f32[2,20,112]{2,0,1:T(2,128)S(1)} %bitcast.87), channel_id=1, replica_groups=mesh['tm'=16,'space'=16] {'space'}, use_global_device_ids=true, to_apply=%region_11.12 | all-reduce | flops 4480 | bytes 35840 | tf_op jit(solution)/shard_map/psum | solution.py:105
  730.2 22.3 %all-gather.5 = f32[16,20,112]{2,1,0:T(8,128)} all-gather(f32[1,20,112]{2,1,0:T(8,128)S(1)} %bitcast.89), channel_id=5, replica_groups=mesh['tm'=16,'space'=16] {'tm'}, dimensions={0}, use_global_device_ids=true | all-gather | bytes 152320 | tf_op jit(solution)/shard_map/all_gather | solution.py:33
  752.5 43.3 %all-gather.11.cloned.1.call-done = f32[320,112,112]{2,1,0:T(8,128)} async-done(((f32[20,112,112]{2,1,0:T(8,128)}), f32[320,112,112]{2,1,0:T(8,128)}) %all-gather.11.cloned.1.call-update) | async-done | bytes 16056336 | tf_op jit(solution)/shard_map/all_gather | solution.py:33
  795.9 33.4 %while.27 = (s32[]{:T(128)}, f32[20,112,112]{2,1,0:T(8,128)S(1)}, f32[20,112]{1,0:T(8,128)S(1)}, s32[]{:T(128)}, f32[16,20,112,112]{3,2,1,0:T(8,128)}, /*index=5...) while((s32[]{:T(128)}, f32[20,112,112]{2,1,0:T(8,128)S(1)}, ...), condition=%wide.region_14.15_spmd, body=%wide.region_13.14_spmd.sunk | while | flops 253126 | bytes 3037603 | solution.py:42
  796.0 1.6 bitcast_add_fusion.10
  797.6 0.7 bitcast_add_fusion.11
  798.3 1.5 bitcast_add_fusion.10
  799.8 0.7 bitcast_add_fusion.11
  800.5 1.5 bitcast_add_fusion.10
  802.0 0.7 bitcast_add_fusion.11
  802.8 1.5 bitcast_add_fusion.10
  804.3 0.7 bitcast_add_fusion.11
  805.0 1.5 bitcast_add_fusion.10
  806.5 0.7 bitcast_add_fusion.11
  807.2 1.5 bitcast_add_fusion.10
  808.7 0.7 bitcast_add_fusion.11
  809.4 1.5 bitcast_add_fusion.10
  810.9 0.7 bitcast_add_fusion.11
  811.6 1.5 bitcast_add_fusion.10
  813.1 0.7 bitcast_add_fusion.11
  813.8 1.5 bitcast_add_fusion.10
  816.1 1.5 bitcast_add_fusion.10
  818.3 1.5 bitcast_add_fusion.10
  820.5 1.5 bitcast_add_fusion.10
  822.0 0.7 bitcast_add_fusion.11
  822.7 1.5 bitcast_add_fusion.10
  824.9 1.5 bitcast_add_fusion.10
  827.1 1.5 bitcast_add_fusion.10
  829.6 5.5 fusion.51
  835.2 1.2 fusion.63
  836.8 2.5 fusion.57
  839.8 1.4 reshape.97
  841.6 1.4 reshape.98
  (96 shorter events, 9.0 us)
Async XLA Ops:
  7.2 127.1 %all-reduce.5.cloned.1.call-start = ((), (), s32[]{:S(2)}) async-start(), calls=%async_computation | async-start | bytes 4587520 | tf_op jit(solution)/shard_map/psum | solution.py:78
  9.2 5.5 copy-start.4
  12.8 1.9 copy-start.6
  14.8 122.6 %copy-start.3 = (bf16[2,2,32,5632]{3,2,1,0:T(8,128)(2,1)S(1)}, bf16[2,2,32,5632]{3,2,1,0:T(8,128)(2,1)}, u32[]{:S(2)}) copy-start(bf16[2,2,32,5632]{3,2,1,0:T(8,128)(2,1)} %param.18) | copy-start | bytes 4325380
  14.8 248.6 %all-gather.9.cloned.1.call-start = ((), (), s32[]{:S(2)}) async-start(), calls=%async_computation.3 | async-start | bytes 19496960 | tf_op jit(solution)/shard_map/all_gather | solution.py:33
  137.2 7.0 copy-start.22
  137.2 7.2 copy-start.17
  137.3 9.2 %copy-start.18 = (bf16[2,2,32,2240]{3,2,1,0:T(8,128)(2,1)S(1)}, bf16[2,2,32,2240]{3,2,1,0:T(8,128)(2,1)}, u32[]{:S(2)}) copy-start(bf16[2,2,32,2240]{3,2,1,0:T(8,128)(2,1)} %param.12) | copy-start | bytes 1720324
  137.3 279.2 %all-reduce.7.cloned.1.call-start = ((), (), s32[]{:S(2)}) async-start(), calls=%async_computation.1 | async-start | bytes 4587520 | tf_op jit(solution)/shard_map/psum | solution.py:105
  138.6 130.2 %collective-permute-start.1 = (bf16[2,1,32,5632]{3,2,1,0:T(8,128)(2,1)}, bf16[2,1,32,5632]{3,2,1,0:T(8,128)(2,1)}, u32[]{:S(2)}, u32[]{:S(2)}) collective-permute-start(bf16[2,1,32,5632]{3,2,1,0:T(8,128)(2,1)} %get-tuple-element.169), channel_id=1, source_target_pairs={{1,0},{2,1},{3,2},{4,3},{5,4},{6,5},{7,6},{8,7},{9,8},{10,9},{11,1... | collective-permute-start | bytes 2162696 | tf_op jit(solution)/shard_map/ppermute | solution.py:22
  140.8 127.9 %collective-permute-start = (bf16[2,1,32,5632]{3,2,1,0:T(8,128)(2,1)}, bf16[2,1,32,5632]{3,2,1,0:T(8,128)(2,1)}, u32[]{:S(2)}, u32[]{:S(2)}) collective-permute-start(bf16[2,1,32,5632]{3,2,1,0:T(8,128)(2,1)} %get-tuple-element.168), channel_id=1, source_target_pairs={{0,1},{1,2},{2,3},{3,4},{4,5},{5,6},{6,7},{7,8},{8,9},{9,10},{10,1... | collective-permute-start | bytes 2162696 | tf_op jit(solution)/shard_map/ppermute | solution.py:20
  148.6 116.3 %copy-start.14 = (bf16[2,64,20,112]{3,2,1,0:T(8,128)(2,1)}, bf16[2,64,20,112]{3,2,1,0:T(8,128)(2,1)S(1)}, u32[]{:S(2)}) copy-start(bf16[2,64,20,112]{3,2,1,0:T(8,128)(2,1)S(1)} %reshape.95) | copy-start | bytes 1720324
  263.8 4.8 copy-start.20
  268.7 401.5 %all-reduce.9.cloned.1.call-start = ((), (), s32[]{:S(2)}) async-start(), calls=%async_computation.2 | async-start | bytes 720896 | tf_op jit(solution)/shard_map/psum | solution.py:137
  268.7 1.9 copy-start.13
  270.6 3.6 copy-start
  276.2 143.3 %copy-start.9 = (f32[2,2,32,2240]{3,2,1,0:T(8,128)S(1)}, f32[2,2,32,2240]{3,2,1,0:T(8,128)}, u32[]{:S(2)}) copy-start(f32[2,2,32,2240]{3,2,1,0:T(8,128)} %get-tuple-element.172) | copy-start | bytes 3440644
  276.2 519.6 %all-gather.11.cloned.1.call-start = ((), (), s32[]{:S(2)}) async-start(), calls=%async_computation.4 | async-start | bytes 19496960 | tf_op jit(solution)/shard_map/all_gather | solution.py:33
  419.5 1.9 copy-start.10
  421.4 1.9 copy-start.19
  423.8 248.1 %copy-start.21 = (f32[2,20,112]{2,0,1:T(2,128)S(1)}, f32[2,20,112]{2,0,1:T(2,128)}, u32[]{:S(2)}) copy-start(f32[2,20,112]{2,0,1:T(2,128)} %copy-done.20) | copy-start | bytes 53764
  423.8 248.1 %copy-start.1 = (f32[2,20,112,112]{3,2,1,0:T(8,128)S(1)}, f32[2,20,112,112]{3,2,1,0:T(8,128)}, u32[]{:S(2)}) copy-start(f32[2,20,112,112]{3,2,1,0:T(8,128)} %all-reduce.5.cloned.1.call-done) | copy-start | bytes 6021124
  671.9 6.7 copy-start.11
  671.9 6.7 copy-start.15
  678.7 1.7 copy-start.12
  683.1 1.9 copy-start.16
  795.9 33.7 %copy-start.2 = (f32[2,20,112,112]{3,2,1,0:T(8,128)S(1)}, f32[2,20,112,112]{3,2,1,0:T(8,128)}, u32[]{:S(2)}) copy-start(f32[2,20,112,112]{3,2,1,0:T(8,128)} %all-reduce.7.cloned.1.call-done) | copy-start | bytes 6021124
  829.6 5.6 copy-start.7
  835.2 1.3 copy-start.5
  835.2 1.6 copy-start.8
Sparse Core Ops, SparseCore 0:
  14.9 119.3 all-reduce.4
  137.4 125.9 all-gather.8
  268.8 147.6 all-reduce.6
  422.5 247.6 all-reduce.8
  672.5 123.2 all-gather.10
where the time goes:
time: 851 us; the launch traced here: 850 us
  waiting for transfers between devices  584 us (69%)
  blocking collectives  134 us (16%)
  other arithmetic  63.2 us (7%)
  matrix products  28.2 us (3%)
  local copies, waits for them, and re-layouts  19.3 us (2%)
  between operations  14.3 us (2%)
    psum x1, waiting for transfers between devices, body(): kernel_total = lax.psum(jnp.stack(kernel_rows), ('tm', 'space'))  234 us
    psum x1, waiting for transfers between devices, body(): grad_states, grad_sums = lax.psum((grad_states, grad_sums), 'space')  140 us
    psum x1, waiting for transfers between devices, body(): states, sums = lax.psum((states, sums), 'space')  119 us
    all_gather x2, waiting for transfers between devices, prefix(): gathered = jax.tree.map(lambda a: lax.all_gather(a, axis), part)  90.5 us
    all_gather x2, blocking collectives, prefix(): gathered = jax.tree.map(lambda a: lax.all_gather(a, axis), part)  45 us
    psum x1, blocking collectives, body(): states, sums = lax.psum((states, sums), 'space')  44.8 us
    psum x1, blocking collectives, body(): grad_states, grad_sums = lax.psum((grad_states, grad_sums), 'space')  44.5 us
    add x30, other arithmetic, add_pair(): return (earlier[0] + later[0], earlier[1] + later[1])  33.3 us
  transfers between devices with their start and end apart: 7, of which 5 were waited for; matrix products, arithmetic and copies ran while one was open for 6% of the time, Pallas kernels for 0%

commit v1 on v0

--- a/solution.py
+++ b/solution.py
@@ -134,7 +134,7 @@
             window = padded[:, 2 - i : 2 - i + rows, 2 - j : 2 - j + cols]
             accum = accum + conv_weight[3 * i + j] * window
             kernel_rows.append(jnp.sum(window * input_wide, axis=(0, 1, 2)))
-    kernel_total = lax.psum(jnp.stack(kernel_rows), ("tm", "space"))
+    kernel_total = lax.psum(lax.psum(jnp.stack(kernel_rows), "space"), "tm")
     tokens_all = frames * rows * cols * lax.axis_size("tm") * lax.axis_size("space")
     kernel_grad = kernel_total * (1.0 / math.sqrt(tokens_all))
     return (

time: 851 us -> 688 us (0.81)
  waiting for transfers between devices: 584 us -> 418 us
    psum x1, waiting for transfers between devices: 234 us -> 0.01 us  [body(): kernel_total = lax.psum(lax.psum(jnp.stack(kernel_rows), 'space'), 'tm')]
    all_gather x2, waiting for transfers between devices: 90.5 us -> 160 us  [prefix(): gathered = jax.tree.map(lambda a: lax.all_gather(a, axis), part)]
  transfers between devices with their start and end apart: 7 -> 7, of which waited for: 5 -> 4; matrix products, arithmetic and copies ran while one was open for 6% -> 7% of each run, Pallas kernels for 0% -> 0%
where the time goes in v1:
time: 688 us; the launch traced here: 686 us
  waiting for transfers between devices  418 us (61%)
  blocking collectives  136 us (20%)
  other arithmetic  63.3 us (9%)
  matrix products  28.2 us (4%)
  local copies, waits for them, and re-layouts  20.9 us (3%)
  between operations  14.3 us (2%)
    all_gather x2, waiting for transfers between devices, prefix(): gathered = jax.tree.map(lambda a: lax.all_gather(a, axis), part)  160 us
    psum x1, waiting for transfers between devices, body(): grad_states, grad_sums = lax.psum((grad_states, grad_sums), 'space')  138 us
    psum x1, waiting for transfers between devices, body(): states, sums = lax.psum((states, sums), 'space')  119 us
    psum x1, blocking collectives, body(): states, sums = lax.psum((states, sums), 'space')  47.3 us
    psum x1, blocking collectives, body(): grad_states, grad_sums = lax.psum((grad_states, grad_sums), 'space')  46.7 us
    all_gather x2, blocking collectives, prefix(): gathered = jax.tree.map(lambda a: lax.all_gather(a, axis), part)  41.5 us
    add x30, other arithmetic, add_pair(): return (earlier[0] + later[0], earlier[1] + later[1])  33.3 us
  transfers between devices with their start and end apart: 7, of which 4 were waited for; matrix products, arithmetic and copies ran while one was open for 7% of the time, Pallas kernels for 0%

profile of v1, /device:TPU:1, one launch (start us, length us, event | category | flops | bytes accessed | tf_op | source)
XLA Modules:
  0.0 686.2 jit_solution(3723952258673597654)
XLA Ops:
  7.2 2.0 reshape.94
  9.2 2.7 convert_reduce_fusion
  12.0 0.8 reshape.93
  12.8 1.9 fusion.78
  14.8 119.5 %all-reduce.6.cloned.1.call-done = f32[2,20,112,112]{3,2,1,0:T(8,128)} async-done(((f32[2,20,112,112]{3,2,1,0:T(8,128)}), f32[2,20,112,112]{3,2,1,0:T(8,128)}) %all-reduce.6.cloned.1.call-update) | async-done | bytes 2007056 | tf_op jit(solution)/shard_map/psum | solution.py:78
  134.3 3.0 reduce_sum.137
  137.3 1.2 fusion.93
  138.5 1.9 collective-permute-start
  140.5 3.3 collective-permute-start.1
  143.9 1.9 reshape.99
  145.8 1.4 fusion.74
  147.2 1.7 reshape.95
  149.0 47.3 %psum.43 = f32[2,20,112]{2,0,1:T(2,128)S(1)} all-reduce(f32[2,20,112]{2,0,1:T(2,128)S(1)} %copy.57), channel_id=1, replica_groups=mesh['tm'=16,'space'=16] {'space'}, use_global_device_ids=true, to_apply=%region_4.5 | all-reduce | flops 4480 | bytes 35840 | tf_op jit(solution)/shard_map/psum | solution.py:78
  196.4 21.1 %all-gather.4 = f32[16,20,112]{2,1,0:T(8,128)S(1)} all-gather(f32[1,20,112]{2,1,0:T(8,128)S(1)} %bitcast.88), channel_id=3, replica_groups=mesh['tm'=16,'space'=16] {'tm'}, dimensions={0}, use_global_device_ids=true | all-gather | bytes 152320 | tf_op jit(solution)/shard_map/all_gather | solution.py:33
  217.6 1.9 maximum_convert_fusion
  219.5 3.6 fusion.8
  223.3 1.6 stack.39
  225.0 38.5 %all-gather.9.cloned.1.call-done = f32[320,112,112]{2,1,0:T(8,128)} async-done(((f32[20,112,112]{2,1,0:T(8,128)}), f32[320,112,112]{2,1,0:T(8,128)}) %all-gather.9.cloned.1.call-update) | async-done | bytes 16056336 | tf_op jit(solution)/shard_map/all_gather | solution.py:33
  263.8 0.8 copy-done.13
  264.6 1.1 fusion.86
  265.7 3.7 fusion.82
  269.5 138.4 %all-reduce.10.cloned.1.call-done = (f32[2,20,112,112]{3,2,1,0:T(8,128)}, f32[9,5632]{1,0:T(8,128)}) async-done(((f32[2,20,112,112]{3,2,1,0:T(8,128)}, f32[9,5632]{1,0:T(8,128)}), (f32[2,20,112,112]{3,2,1,0:T(8,128)}, f32[9,5632]{1,0:T(8,128)})) %all-reduce.10.cloned.1.call-update) | async-done | bytes 2209808 | tf_op jit(solution)/shard_map/psum | solution.py:105
  408.2 3.0 reduce_sum.142
  411.2 1.9 select_n.43
  413.1 2.0 select_n.45
  415.6 12.4 %add_convert_fusion = bf16[2,2,32,5632]{3,2,1,0:T(8,128)(2,1)} fusion(f32[2,4,32,5632]{3,2,1,0:T(8,128)} %copy-done, f32[5632]{0:T(1024)S(1)} %get-tuple-element.140, f32[5632]{0:T(1024)S(1)} %get-tuple-element.141, f32[5632]{0:T(1024)S(1)} %get-tuple-element.134, f32[5632]{0:T(1024)S(1)} %get-tuple-element.135, f32[5632]{0:T(1024)S(1)} %get-tuple-element.136, ...), kind=kLoop, calls=%fused_computation.29 | loop fusion | flops 12976128 | bytes 16062464 | tf_op jit(solution)/shard_map/convert_element_type | solution.py:144
  428.1 6.7 fusion.48
  434.8 1.6 fusion.66
  437.1 2.8 fusion.54
  440.3 1.4 reshape.96
  441.7 46.7 %psum.45 = f32[2,20,112]{2,0,1:T(2,128)S(1)} all-reduce(f32[2,20,112]{2,0,1:T(2,128)S(1)} %bitcast.87), channel_id=1, replica_groups=mesh['tm'=16,'space'=16] {'space'}, use_global_device_ids=true, to_apply=%region_11.12 | all-reduce | flops 4480 | bytes 35840 | tf_op jit(solution)/shard_map/psum | solution.py:105
  488.5 20.3 %all-gather.5 = f32[16,20,112]{2,1,0:T(8,128)} all-gather(f32[1,20,112]{2,1,0:T(8,128)S(1)} %bitcast.89), channel_id=5, replica_groups=mesh['tm'=16,'space'=16] {'tm'}, dimensions={0}, use_global_device_ids=true | all-gather | bytes 152320 | tf_op jit(solution)/shard_map/all_gather | solution.py:33
  508.8 1.8 broadcast_multiply_fusion
  510.6 121.6 %all-gather.11.cloned.1.call-done = f32[320,112,112]{2,1,0:T(8,128)} async-done(((f32[20,112,112]{2,1,0:T(8,128)}), f32[320,112,112]{2,1,0:T(8,128)}) %all-gather.11.cloned.1.call-update) | async-done | bytes 16056336 | tf_op jit(solution)/shard_map/all_gather | solution.py:33
  632.3 33.7 %while.27 = (s32[]{:T(128)}, f32[20,112,112]{2,1,0:T(8,128)S(1)}, f32[20,112]{1,0:T(8,128)S(1)}, s32[]{:T(128)}, f32[16,20,112,112]{3,2,1,0:T(8,128)}, /*index=5...) while((s32[]{:T(128)}, f32[20,112,112]{2,1,0:T(8,128)S(1)}, ...), condition=%wide.region_14.15_spmd, body=%wide.region_13.14_spmd.sunk | while | flops 253126 | bytes 3037603 | solution.py:42
  632.3 0.9 bitcast_add_fusion.11
  633.2 1.5 bitcast_add_fusion.10
  634.7 0.7 bitcast_add_fusion.11
  635.4 1.5 bitcast_add_fusion.10
  637.0 0.7 bitcast_add_fusion.11
  637.7 1.5 bitcast_add_fusion.10
  639.2 0.7 bitcast_add_fusion.11
  639.9 1.5 bitcast_add_fusion.10
  642.1 1.5 bitcast_add_fusion.10
  644.4 1.5 bitcast_add_fusion.10
  645.9 0.7 bitcast_add_fusion.11
  646.6 1.5 bitcast_add_fusion.10
  648.1 0.7 bitcast_add_fusion.11
  648.8 1.5 bitcast_add_fusion.10
  650.4 0.7 bitcast_add_fusion.11
  651.1 1.5 bitcast_add_fusion.10
  652.6 0.7 bitcast_add_fusion.11
  653.3 1.5 bitcast_add_fusion.10
  654.8 0.7 bitcast_add_fusion.11
  655.5 1.5 bitcast_add_fusion.10
  657.8 1.5 bitcast_add_fusion.10
  660.0 1.5 bitcast_add_fusion.10
  662.2 1.5 bitcast_add_fusion.10
  664.5 1.5 bitcast_add_fusion.10
  666.2 5.5 fusion.51
  671.8 1.2 fusion.63
  673.4 2.5 fusion.57
  676.4 1.4 reshape.97
  678.3 1.4 reshape.98
  (90 shorter events, 8.9 us)
Async XLA Ops:
  7.2 127.1 %all-reduce.6.cloned.1.call-start = ((), (), s32[]{:S(2)}) async-start(), calls=%async_computation | async-start | bytes 4587520 | tf_op jit(solution)/shard_map/psum | solution.py:78
  9.2 5.5 copy-start.4
  12.8 1.9 copy-start.6
  14.8 122.6 %copy-start.3 = (bf16[2,2,32,5632]{3,2,1,0:T(8,128)(2,1)S(1)}, bf16[2,2,32,5632]{3,2,1,0:T(8,128)(2,1)}, u32[]{:S(2)}) copy-start(bf16[2,2,32,5632]{3,2,1,0:T(8,128)(2,1)} %param.18) | copy-start | bytes 4325380
  14.8 248.6 %all-gather.9.cloned.1.call-start = ((), (), s32[]{:S(2)}) async-start(), calls=%async_computation.2 | async-start | bytes 19496960 | tf_op jit(solution)/shard_map/all_gather | solution.py:33
  137.2 6.5 copy-start.19
  137.2 6.7 copy-start.15
  137.3 270.7 %all-reduce.10.cloned.1.call-start = ((), (), s32[]{:S(2)}) async-start(), calls=%async_computation.4 | async-start | bytes 5308416 | tf_op jit(solution)/shard_map/psum | solution.py:105
  138.5 79.0 %collective-permute-start = (bf16[2,1,32,5632]{3,2,1,0:T(8,128)(2,1)}, bf16[2,1,32,5632]{3,2,1,0:T(8,128)(2,1)}, u32[]{:S(2)}, u32[]{:S(2)}) collective-permute-start(bf16[2,1,32,5632]{3,2,1,0:T(8,128)(2,1)} %get-tuple-element.170), channel_id=1, source_target_pairs={{0,1},{1,2},{2,3},{3,4},{4,5},{5,6},{6,7},{7,8},{8,9},{9,10},{10,1... | collective-permute-start | bytes 2162696 | tf_op jit(solution)/shard_map/ppermute | solution.py:20
  140.5 77.1 %collective-permute-start.1 = (bf16[2,1,32,5632]{3,2,1,0:T(8,128)(2,1)}, bf16[2,1,32,5632]{3,2,1,0:T(8,128)(2,1)}, u32[]{:S(2)}, u32[]{:S(2)}) collective-permute-start(bf16[2,1,32,5632]{3,2,1,0:T(8,128)(2,1)} %get-tuple-element.171), channel_id=1, source_target_pairs={{1,0},{2,1},{3,2},{4,3},{5,4},{6,5},{7,6},{8,7},{9,8},{10,9},{11,1... | collective-permute-start | bytes 2162696 | tf_op jit(solution)/shard_map/ppermute | solution.py:22
  217.5 1.9 copy-start.12
  219.4 3.6 copy-start
  263.5 1.1 copy-start.13
  263.8 5.6 copy-start.17
  269.5 239.4 %all-reduce.8.cloned.1.call-start = ((), (), s32[]{:S(2)}) async-start(), calls=%async_computation.1 | async-start | bytes 720896 | tf_op jit(solution)/shard_map/psum | solution.py:137
  408.0 224.3 %all-gather.11.cloned.1.call-start = ((), (), s32[]{:S(2)}) async-start(), calls=%async_computation.3 | async-start | bytes 19496960 | tf_op jit(solution)/shard_map/all_gather | solution.py:33
  411.2 1.9 copy-start.9
  413.1 2.0 copy-start.16
  415.6 12.4 %copy-start.18 = (f32[2,20,112]{2,0,1:T(2,128)S(1)}, f32[2,20,112]{2,0,1:T(2,128)}, u32[]{:S(2)}) copy-start(f32[2,20,112]{2,0,1:T(2,128)} %copy-done.17) | copy-start | bytes 53764
  415.6 12.4 %copy-start.1 = (f32[2,20,112,112]{3,2,1,0:T(8,128)S(1)}, f32[2,20,112,112]{3,2,1,0:T(8,128)}, u32[]{:S(2)}) copy-start(f32[2,20,112,112]{3,2,1,0:T(8,128)} %all-reduce.6.cloned.1.call-done) | copy-start | bytes 6021124
  428.0 6.7 copy-start.10
  428.1 6.7 copy-start.14
  434.8 2.3 copy-start.11
  632.3 33.9 %copy-start.2 = (f32[2,20,112,112]{3,2,1,0:T(8,128)S(1)}, f32[2,20,112,112]{3,2,1,0:T(8,128)}, u32[]{:S(2)}) copy-start(f32[2,20,112,112]{3,2,1,0:T(8,128)} %get-tuple-element.166) | copy-start | bytes 6021124
  666.2 5.6 copy-start.7
  671.8 1.3 copy-start.5
  671.8 1.6 copy-start.8
Sparse Core Ops, SparseCore 0:
  14.9 119.3 all-reduce.5
  137.4 125.9 all-gather.8
  269.6 138.2 all-reduce.9
  411.4 93.6 all-reduce.7
  507.7 124.4 all-gather.10
